TPU v7x, 32 devices: a whole 2x2x4 slice. The times are simulated.
32 devices in a mesh: dp: 4 (over y, x), expert: 8 (over z, core).
Axes of the slice: x: 2, y: 2, z: 4, core: 2. Of those that a mesh axis runs over, the one named last changes fastest.
Arguments:
- tokens: bfloat16 [4096, 2560], P(('dp', 'expert')), may hold values from -6 to 6
- routes: int32 [4096, 2], P(('dp', 'expert')), may hold values from 0 to 7, all different within a row; in each aligned block of 128 rows (0 to 127, 128 to 255, ...) at most 36 rows name the same one
- route_gates: float32 [4096, 2], P(('dp', 'expert')), may hold values from 0.2 to 1
- w_gate: bfloat16 [8, 2560, 768], P('expert', 'dp'), may hold values from -0.125 to 0.125
- w_up: bfloat16 [8, 2560, 768], P('expert', 'dp'), may hold values from -0.125 to 0.125
- w_down: bfloat16 [8, 768, 2560], P('expert', None, 'dp'), may hold values from -0.21875 to 0.21875
- cotangent: bfloat16 [4096, 2560], P(('dp', 'expert')), may hold values from -6 to 6
Outputs:
- layer_out: bfloat16 [4096, 2560], P(('dp', 'expert'))
- token_grad: bfloat16 [4096, 2560], P(('dp', 'expert'))
- gate_grad: float32 [4096, 2], P(('dp', 'expert'))
Inputs may be any that keep to these rules, and one draw needn't show every extreme that they name: `routes`: among the 128 rows of one device, each expert is named at most 36 times, and in every draw some device names some expert exactly 36 times. The 2 experts of a token differ.
All inputs are finite; a program needn't handle non-finite values.
Results may differ from a plain program's by a relative error of at most 0.0067.
Values may be sent and summed in bfloat16 or wider, within the bound.
A program may use at most 128 MiB of HBM per device.

v0:
```python
import jax
import jax.numpy as jnp
from jax import lax
from jax.sharding import PartitionSpec as P

EXP_DEV = 1


def expert_forward(arriving, gate_full, up_full, down_full):
    gate_pre = jnp.einsum("snd,df->snf", arriving, gate_full, preferred_element_type=jnp.float32)
    up_pre = jnp.einsum("snd,df->snf", arriving, up_full, preferred_element_type=jnp.float32)
    hidden = (gate_pre * jax.nn.sigmoid(gate_pre) * up_pre).astype(jnp.bfloat16)
    expert_out = jnp.einsum(
        "snf,fd->snd", hidden, down_full, preferred_element_type=jnp.float32
    ).astype(jnp.bfloat16)
    return (expert_out, gate_pre, up_pre)


def expert_backward(arriving_grad, gate_pre, up_pre, gate_full, up_full, down_full):
    hidden_grad = jnp.einsum(
        "snd,fd->snf", arriving_grad, down_full, preferred_element_type=jnp.float32
    )
    logistic = jax.nn.sigmoid(gate_pre)
    pre_gate = (hidden_grad * up_pre * logistic * (1.0 + gate_pre * (1.0 - logistic))).astype(
        jnp.bfloat16
    )
    pre_up = (hidden_grad * gate_pre * logistic).astype(jnp.bfloat16)
    input_grad = jnp.einsum("snf,df->snd", pre_gate, gate_full, preferred_element_type=jnp.float32)
    input_grad = input_grad + jnp.einsum(
        "snf,df->snd", pre_up, up_full, preferred_element_type=jnp.float32
    )
    return input_grad.astype(jnp.bfloat16)


def local(tokens, routes, route_gates, w_gate, w_up, w_down, cotangent):
    groups = lax.axis_size("expert")
    tok_rows = tokens.shape[0]
    top_count = routes.shape[1]
    width = tokens.shape[1]
    capacity = 9 * tok_rows * top_count // (8 * groups * EXP_DEV)
    pair_expert = routes.reshape(-1)
    pair_token = jnp.arange(tok_rows * top_count, dtype=jnp.int32) // top_count
    onehot = (pair_expert[:, None] == jnp.arange(groups, dtype=jnp.int32)[None, :]).astype(
        jnp.int32
    )
    slot_rank = jnp.sum((jnp.cumsum(onehot, axis=0) - onehot) * onehot, axis=1)
    slot_place = pair_expert * capacity + slot_rank
    outbox = (
        jnp.zeros((groups * capacity, width), jnp.bfloat16).at[slot_place].set(tokens[pair_token])
    )
    outbox = outbox.reshape(groups, capacity, width)
    pair_gate = route_gates.reshape(-1)
    cot_pairs = cotangent[pair_token].astype(jnp.float32)
    row_grad = (pair_gate[:, None] * cot_pairs).astype(jnp.bfloat16)
    gradbox = jnp.zeros((groups * capacity, width), jnp.bfloat16).at[slot_place].set(row_grad)
    gradbox = gradbox.reshape(groups, capacity, width)
    gate_full, up_full, down_full = (
        lax.all_gather(w_gate[0], "dp", axis=0, tiled=True),
        lax.all_gather(w_up[0], "dp", axis=0, tiled=True),
        lax.all_gather(w_down[0], "dp", axis=1, tiled=True),
    )
    expert_out, gate_pre, up_pre = expert_forward(
        lax.all_to_all(outbox, "expert", split_axis=0, concat_axis=0, tiled=True),
        gate_full,
        up_full,
        down_full,
    )
    returned = lax.all_to_all(expert_out, "expert", split_axis=0, concat_axis=0, tiled=True)
    returned, gate_pre, up_pre = (returned, gate_pre, up_pre)
    arriving_grad = lax.all_to_all(gradbox, "expert", split_axis=0, concat_axis=0, tiled=True)
    input_grad = expert_backward(arriving_grad, gate_pre, up_pre, gate_full, up_full, down_full)
    back_grad = lax.all_to_all(input_grad, "expert", split_axis=0, concat_axis=0, tiled=True)
    pair_out = returned.reshape(groups * capacity, width)[slot_place].astype(jnp.float32)
    layer_out = jnp.sum(
        (pair_gate[:, None] * pair_out).reshape(tok_rows, top_count, width), axis=1
    ).astype(jnp.bfloat16)
    gate_grad = jnp.sum(cot_pairs * pair_out, axis=1).reshape(tok_rows, top_count)
    pair_grad = back_grad.reshape(groups * capacity, width)[slot_place].astype(jnp.float32)
    token_grad = jnp.sum(pair_grad.reshape(tok_rows, top_count, width), axis=1).astype(jnp.bfloat16)
    return (layer_out, token_grad, gate_grad)


def solution(mesh):
    in_specs = (
        P(("dp", "expert"), None),
        P(("dp", "expert"), None),
        P(("dp", "expert"), None),
        P("expert", "dp", None),
        P("expert", "dp", None),
        P("expert", None, "dp"),
        P(("dp", "expert"), None),
    )
    out_specs = (P(("dp", "expert"), None), P(("dp", "expert"), None), P(("dp", "expert"), None))
    return jax.shard_map(local, mesh=mesh, in_specs=in_specs, out_specs=out_specs, check_vma=False)
```

profile of v0, /device:TPU:0, one launch (start us, length us, event | category | flops | bytes accessed | tf_op | source)
XLA Modules:
  0.0 285.9 jit_solution(3171517548182173325)
XLA Ops:
  7.2 0.0 copy-start
  7.2 0.0 copy-start.4
  7.2 0.0 all-gather.7.cloned.1.call-start
  7.2 0.7 all-gather.7.cloned.1.call-update
  7.9 0.0 all-gather.9.cloned.1.call-start
  8.0 0.7 all-gather.9.cloned.1.call-update
  8.7 0.0 all-gather.11.cloned.1.call-start
  8.7 0.7 all-gather.11.cloned.1.call-update
  9.4 0.0 copy-done.4
  9.4 0.1 copy.13
  9.5 0.1 eq.29
  9.7 0.1 eq.25
  9.8 0.1 copy.12
  9.9 0.1 mul.68
  10.1 0.6 reduce-window.6
  10.7 0.2 slice_reduce_fusion
  11.0 0.1 fusion.24
  11.1 0.0 copy-done
  11.1 6.9 %scatter_custom_fusion = bf16[288,2560]{1,0:T(8,128)(2,1)S(1)} fusion(s32[256]{0:T(256)S(1)} %bitcast.34, bf16[128,2560]{1,0:T(8,128)(2,1)S(1)} %copy-done, s32[1024]{0:T(1024)S(1)} %pad_clamp_fusion.1, bf16[]{:T(256)} %constant.26.clone.1), kind=kCustom, calls=%fused_computation.25 | custom fusion | bytes 1474562 | tf_op jit(solution)/shard_map/scatter | solution.py:49
  18.0 1.4 reshape.123
  19.3 0.0 copy-start.5
  19.3 0.0 copy-start.1
  19.3 6.5 %all-to-all-start = ((bf16[8,36,2560]{2,1,0:T(8,128)(2,1)}), bf16[8,36,2560]{2,1,0:T(8,128)(2,1)}, u32[]{:S(2)}, u32[]{:S(2)}) async-start(bf16[8,36,2560]{2,1,0:T(8,128)(2,1)} %reshape.123), calls=%async_computation | async-start | bytes 3276800 | tf_op jit(solution)/shard_map/all_to_all | solution.py:63
  25.8 0.0 copy-done.5
  25.8 0.1 copy.11
  25.9 0.1 mul.73
  26.0 0.0 copy-done.1
  26.1 1.4 gather_fusion.1
  27.5 3.1 %scatter_custom_fusion.1 = bf16[288,2560]{1,0:T(8,128)(2,1)S(1)} fusion(s32[256]{0:T(256)S(1)} %bitcast.35, bf16[256,2560]{1,0:T(8,128)(2,1)S(1)} %gather_fusion.1, f32[256]{0:T(256)S(1)} %mul.73, bf16[]{:T(256)} %constant.26.clone.1), kind=kCustom, calls=%fused_computation.24 | custom fusion | flops 1966080 | bytes 2786306 | tf_op jit(solution)/shard_map/scatter | solution.py:55
  30.6 1.4 reshape.125
  32.1 33.1 %all-to-all-done = bf16[8,36,2560]{2,1,0:T(8,128)(2,1)} async-done(((bf16[8,36,2560]{2,1,0:T(8,128)(2,1)}), bf16[8,36,2560]{2,1,0:T(8,128)(2,1)}, u32[]{:S(2)}, u32[]{:S(2)}) %all-to-all-start) | async-done | bytes 1474592 | tf_op jit(solution)/shard_map/all_to_all | solution.py:63
  65.1 4.3 %all-to-all-start.2 = ((bf16[8,36,2560]{2,1,0:T(8,128)(2,1)}), bf16[8,36,2560]{2,1,0:T(8,128)(2,1)}, u32[]{:S(2)}, u32[]{:S(2)}) async-start(bf16[8,36,2560]{2,1,0:T(8,128)(2,1)} %reshape.125), calls=%async_computation.2 | async-start | bytes 3276800 | tf_op jit(solution)/shard_map/all_to_all | solution.py:70
  69.4 0.0 all-gather.7.cloned.1.call-done
  69.5 4.3 %fusion.9 = f32[8,36,768]{2,1,0:T(8,128)S(1)} fusion(bf16[8,36,2560]{2,1,0:T(8,128)(2,1)} %all-to-all-done, bf16[1,2560,768]{2,1,0:T(8,128)(2,1)} %all-gather.7.cloned.1.call-done), kind=kOutput, calls=%fused_computation.17 | convolution fusion | flops 1132462080 | bytes 6291456 | tf_op jit(solution)/shard_map/snd,df->snf/dot_general | solution.py:10
  73.8 41.8 %all-gather.9.cloned.1.call-done = bf16[1,2560,768]{2,1,0:T(8,128)(2,1)} async-done(((bf16[1,640,768]{2,1,0:T(8,128)(2,1)}), bf16[1,2560,768]{2,1,0:T(8,128)(2,1)}) %all-gather.9.cloned.1.call-update) | async-done | bytes 3932176 | tf_op jit(solution)/shard_map/all_gather | solution.py:59
  115.5 5.0 %fusion.5 = f32[8,36,768]{2,1,0:T(8,128)} fusion(bf16[8,36,2560]{2,1,0:T(8,128)(2,1)} %all-to-all-done, bf16[1,2560,768]{2,1,0:T(8,128)(2,1)} %all-gather.9.cloned.1.call-done), kind=kOutput, calls=%fused_computation.13 | convolution fusion | flops 1132462080 | bytes 6291456 | tf_op jit(solution)/shard_map/snd,df->snf/dot_general | solution.py:11
  120.6 47.4 %all-gather.11.cloned.1.call-done = bf16[1,768,2560]{2,1,0:T(8,128)(2,1)} async-done(((bf16[1,768,640]{2,1,0:T(8,128)(2,1)}), bf16[1,768,2560]{2,1,0:T(8,128)(2,1)}) %all-gather.11.cloned.1.call-update) | async-done | bytes 3932176 | tf_op jit(solution)/shard_map/all_gather | solution.py:60
  167.9 5.1 %convolution_convert_fusion = bf16[8,36,2560]{2,1,0:T(8,128)(2,1)} fusion(bf16[1,768,2560]{2,1,0:T(8,128)(2,1)} %all-gather.11.cloned.1.call-done, f32[8,36,768]{2,1,0:T(8,128)} %fusion.5, f32[8,36,768]{2,1,0:T(8,128)S(1)} %fusion.9), kind=kOutput, calls=%fused_computation.8 | convolution fusion | flops 1134526464 | bytes 7176192 | tf_op jit(solution)/shard_map/snf,fd->snd/dot_general | solution.py:13
  173.0 0.0 all-to-all-done.2
  173.0 4.6 %all-to-all-start.1 = ((bf16[8,36,2560]{2,1,0:T(8,128)(2,1)}), bf16[8,36,2560]{2,1,0:T(8,128)(2,1)}, u32[]{:S(2)}, u32[]{:S(2)}) async-start(bf16[8,36,2560]{2,1,0:T(8,128)(2,1)} %convolution_convert_fusion), calls=%async_computation.1 | async-start | bytes 3276800 | tf_op jit(solution)/shard_map/all_to_all | solution.py:68
  177.7 0.0 copy-start.8
  177.7 4.2 %fusion.1 = f32[8,36,768]{2,1,0:T(8,128)S(1)} fusion(bf16[8,36,2560]{2,1,0:T(8,128)(2,1)} %all-to-all-done.2, bf16[1,768,2560]{2,1,0:T(8,128)(2,1)} %all-gather.11.cloned.1.call-done), kind=kOutput, calls=%fused_computation.9 | convolution fusion | flops 1132462080 | bytes 6291456 | tf_op jit(solution)/shard_map/snd,fd->snf/dot_general | solution.py:20
  181.9 0.0 copy-done.6
  181.9 0.0 copy-done.8
  181.9 0.0 copy-start.7
  181.9 1.7 fusion.7
  183.6 0.4 copy-done.7
  184.0 2.7 fusion
  186.8 30.2 %all-to-all-done.1 = bf16[8,36,2560]{2,1,0:T(8,128)(2,1)} async-done(((bf16[8,36,2560]{2,1,0:T(8,128)(2,1)}), bf16[8,36,2560]{2,1,0:T(8,128)(2,1)}, u32[]{:S(2)}, u32[]{:S(2)}) %all-to-all-start.1) | async-done | bytes 1474592 | tf_op jit(solution)/shard_map/all_to_all | solution.py:68
  217.0 4.3 %all-to-all-start.3 = ((bf16[8,36,2560]{2,1,0:T(8,128)(2,1)}), bf16[8,36,2560]{2,1,0:T(8,128)(2,1)}, u32[]{:S(2)}, u32[]{:S(2)}) async-start(bf16[8,36,2560]{2,1,0:T(8,128)(2,1)} %fusion), calls=%async_computation.3 | async-start | bytes 3276800 | tf_op jit(solution)/shard_map/all_to_all | solution.py:72
  221.3 1.6 reshape.124
  222.9 2.5 gather_fusion
  225.4 4.2 %reshape.128 = f32[128,2,2560]{2,1,0:T(2,128)} reshape(bf16[256,2560]{1,0:T(8,128)(2,1)} %gather_fusion) | data formatting | bytes 3932160 | tf_op jit(solution)/shard_map/convert_element_type | solution.py:73
  229.6 0.0 copy-done.2
  229.6 0.4 fusion.12
  230.1 30.5 %all-to-all-done.3 = bf16[8,36,2560]{2,1,0:T(8,128)(2,1)} async-done(((bf16[8,36,2560]{2,1,0:T(8,128)(2,1)}), bf16[8,36,2560]{2,1,0:T(8,128)(2,1)}, u32[]{:S(2)}, u32[]{:S(2)}) %all-to-all-start.3) | async-done | bytes 1474592 | tf_op jit(solution)/shard_map/all_to_all | solution.py:72
  260.5 1.5 reshape.126
  262.1 2.5 gather_fusion.2
  264.6 4.1 %gather.18 = bf16[128,2,2560]{2,1,0:T(2,128)(2,1)} reshape(bf16[256,2560]{1,0:T(8,128)(2,1)} %gather_fusion.2) | data formatting | bytes 2621440 | tf_op jit(solution)/shard_map/gather | solution.py:78
  268.7 5.3 %reduce_sum.44 = bf16[128,2560]{1,0:T(8,128)(2,1)} reduce(bf16[128,2,2560]{2,1,0:T(2,128)(2,1)} %gather.18, bf16[]{:T(256)} %constant.26.clone.1), dimensions={1}, to_apply=%region_6.7 | reduce | flops 327680 | bytes 1966082 | tf_op jit(solution)/shard_map/reduce_sum | solution.py:79
  274.0 0.1 reshape.127
  274.2 0.6 copy.16
  274.8 0.0 copy-done.3
  274.8 4.5 %multiply_reduce_fusion = bf16[128,2560]{1,0:T(8,128)(2,1)} fusion(f32[128,2,2560]{2,1,0:T(2,128)S(1)} %copy-done.3, f32[128,2]{1,0:T(8,128)S(1)} %copy.11), kind=kLoop, calls=%fused_computation.23 | loop fusion | flops 983040 | bytes 3277824 | tf_op jit(solution)/shard_map/reduce_sum | solution.py:74
  (11 shorter events, 0.1 us)
Async XLA Ops:
  7.2 3.9 %copy-start = (bf16[128,2560]{1,0:T(8,128)(2,1)S(1)}, bf16[128,2560]{1,0:T(8,128)(2,1)}, u32[]{:S(2)}) copy-start(bf16[128,2560]{1,0:T(8,128)(2,1)} %param.7) | copy-start | bytes 1966084
  7.2 2.2 copy-start.4
  7.2 62.3 %all-gather.7.cloned.1.call-start = ((), (), s32[]{:S(2)}) async-start(), calls=%async_computation.4 | async-start | bytes 4915200 | tf_op jit(solution)/shard_map/all_gather | solution.py:58
  7.9 107.6 %all-gather.9.cloned.1.call-start = ((), (), s32[]{:S(2)}) async-start(), calls=%async_computation.5 | async-start | bytes 4915200 | tf_op jit(solution)/shard_map/all_gather | solution.py:59
  8.7 159.3 %all-gather.11.cloned.1.call-start = ((), (), s32[]{:S(2)}) async-start(), calls=%async_computation.6 | async-start | bytes 4915200 | tf_op jit(solution)/shard_map/all_gather | solution.py:60
  19.3 6.5 %copy-start.5 = (f32[128,2]{0,1:T(2,128)S(1)}, f32[128,2]{0,1:T(2,128)}, u32[]{:S(2)}) copy-start(f32[128,2]{0,1:T(2,128)} %param.9) | copy-start | bytes 3076
  19.3 6.7 %copy-start.1 = (bf16[128,2560]{1,0:T(8,128)(2,1)S(1)}, bf16[128,2560]{1,0:T(8,128)(2,1)}, u32[]{:S(2)}) copy-start(bf16[128,2560]{1,0:T(8,128)(2,1)} %param.13) | copy-start | bytes 1966084
  19.3 45.8 %all-to-all-start = ((bf16[8,36,2560]{2,1,0:T(8,128)(2,1)}), bf16[8,36,2560]{2,1,0:T(8,128)(2,1)}, u32[]{:S(2)}, u32[]{:S(2)}) async-start(bf16[8,36,2560]{2,1,0:T(8,128)(2,1)} %reshape.123), calls=%async_computation | async-start | bytes 3276800 | tf_op jit(solution)/shard_map/all_to_all | solution.py:63
  65.1 107.9 %all-to-all-start.2 = ((bf16[8,36,2560]{2,1,0:T(8,128)(2,1)}), bf16[8,36,2560]{2,1,0:T(8,128)(2,1)}, u32[]{:S(2)}, u32[]{:S(2)}) async-start(bf16[8,36,2560]{2,1,0:T(8,128)(2,1)} %reshape.125), calls=%async_computation.2 | async-start | bytes 3276800 | tf_op jit(solution)/shard_map/all_to_all | solution.py:70
  173.0 43.9 %all-to-all-start.1 = ((bf16[8,36,2560]{2,1,0:T(8,128)(2,1)}), bf16[8,36,2560]{2,1,0:T(8,128)(2,1)}, u32[]{:S(2)}, u32[]{:S(2)}) async-start(bf16[8,36,2560]{2,1,0:T(8,128)(2,1)} %convolution_convert_fusion), calls=%async_computation.1 | async-start | bytes 3276800 | tf_op jit(solution)/shard_map/all_to_all | solution.py:68
  177.7 4.3 %copy-start.6 = (bf16[1,2560,768]{2,1,0:T(8,128)(2,1)S(1)}, bf16[1,2560,768]{2,1,0:T(8,128)(2,1)}, u32[]{:S(2)}) copy-start(bf16[1,2560,768]{2,1,0:T(8,128)(2,1)} %all-gather.7.cloned.1.call-done) | copy-start | bytes 11796484
  177.7 4.3 %copy-start.8 = (f32[8,36,768]{2,1,0:T(8,128)S(1)}, f32[8,36,768]{2,1,0:T(8,128)}, u32[]{:S(2)}) copy-start(f32[8,36,768]{2,1,0:T(8,128)} %fusion.5) | copy-start | bytes 2654212
  181.9 2.1 copy-start.7
  217.0 43.5 %all-to-all-start.3 = ((bf16[8,36,2560]{2,1,0:T(8,128)(2,1)}), bf16[8,36,2560]{2,1,0:T(8,128)(2,1)}, u32[]{:S(2)}, u32[]{:S(2)}) async-start(bf16[8,36,2560]{2,1,0:T(8,128)(2,1)} %fusion), calls=%async_computation.3 | async-start | bytes 3276800 | tf_op jit(solution)/shard_map/all_to_all | solution.py:72
  225.4 4.2 %copy-start.2 = (bf16[256,2560]{1,0:T(8,128)(2,1)S(1)}, bf16[256,2560]{1,0:T(8,128)(2,1)}, u32[]{:S(2)}) copy-start(bf16[256,2560]{1,0:T(8,128)(2,1)} %gather_fusion) | copy-start | bytes 3932164
  264.6 10.2 %copy-start.3 = (f32[128,2,2560]{2,1,0:T(2,128)S(1)}, f32[128,2,2560]{2,1,0:T(2,128)}, u32[]{:S(2)}) copy-start(f32[128,2,2560]{2,1,0:T(2,128)} %reshape.128) | copy-start | bytes 7864324
Sparse Core Ops, SparseCore 0:
  9.9 53.2 all-gather.6
  65.0 50.5 all-gather.8
  117.4 50.5 all-gather.10
where the time goes:
time: 286 us
  waiting for transfers between devices  185 us (65%)
  local copies, waits for them, and re-layouts  29.9 us (10%)
  matrix products  23.1 us (8%)
  starting transfers between devices  19.8 us (7%)
  other arithmetic  14.1 us (5%)
  between operations  14 us (5%)
    all_gather x1, waiting for transfers between devices, local(): lax.all_gather(w_down[0], 'dp', axis=1, tiled=True)  47.4 us
    all_gather x1, waiting for transfers between devices, local(): lax.all_gather(w_up[0], 'dp', axis=0, tiled=True)  41.8 us
    all_to_all x1, waiting for transfers between devices, local(): lax.all_to_all(outbox, 'expert', split_axis=0, concat_axis=0, tiled=True)  33.1 us
    all_to_all x1, waiting for transfers between devices, local(): lax.all_to_all(input_grad, 'expert', split_axis=0, concat_axis=0, tiled=T...  30.5 us
    all_to_all x1, waiting for transfers between devices, local(): lax.all_to_all(expert_out, 'expert', split_axis=0, concat_axis=0, tiled=T...  30.2 us
    scatter x1, local copies, waits for them, and re-layouts, local(): jnp.zeros((groups * capacity, width), jnp.bfloat16).at[slot_place]  6.87 us
    gather x2, local copies, waits for them, and re-layouts, local(): back_grad.reshape(groups * capacity, width)[slot_place].astype(jnp.float32)  6.62 us
    all_to_all x1, starting transfers between devices, local(): lax.all_to_all(outbox, 'expert', split_axis=0, concat_axis=0, tiled=True)  6.46 us
  transfers between devices with their start and end apart: 7, of which 5 were waited for; matrix products, arithmetic and copies ran while one was open for 17% of the time, Pallas kernels for 0%

commit v1 on v0

--- a/solution.py
+++ b/solution.py
@@ -4,6 +4,18 @@
 from jax.sharding import PartitionSpec as P
 
 EXP_DEV = 1
+
+
+def gather_by_bits(shard, axis, dim):
+    ways, here = (lax.axis_size(axis), lax.axis_index(axis))
+    grown, reach = (shard, 1)
+    while reach < ways:
+        theirs = lax.ppermute(grown, axis, [(d, d ^ reach) for d in range(ways)])
+        mine_first = jnp.concatenate([grown, theirs], axis=dim)
+        theirs_first = jnp.concatenate([theirs, grown], axis=dim)
+        grown = jnp.where(here & reach == 0, mine_first, theirs_first)
+        reach = 2 * reach
+    return grown
 
 
 def expert_forward(arriving, gate_full, up_full, down_full):
@@ -57,7 +69,7 @@
     gate_full, up_full, down_full = (
         lax.all_gather(w_gate[0], "dp", axis=0, tiled=True),
         lax.all_gather(w_up[0], "dp", axis=0, tiled=True),
-        lax.all_gather(w_down[0], "dp", axis=1, tiled=True),
+        gather_by_bits(w_down[0], "dp", 1),
     )
     expert_out, gate_pre, up_pre = expert_forward(
         lax.all_to_all(outbox, "expert", split_axis=0, concat_axis=0, tiled=True),

time: 286 us -> 268 us (0.937)
  waiting for transfers between devices: 185 us -> 157 us
  starting transfers between devices: 19.8 us -> 23.1 us
  other arithmetic: 14.1 us -> 17.3 us
    all_gather x1 -> x0, waiting for transfers between devices: 47.4 us -> none  [local(): lax.all_gather(w_down[0], 'dp', axis=1, tiled=True)]
    ppermute x0 -> x2, waiting for transfers between devices: none -> 36.3 us  [gather_by_bits(): theirs = lax.ppermute(grown, axis, [(d, d ^ reach) for d in range(ways)])]
    all_to_all x1, waiting for transfers between devices: 33.1 us -> 0.01 us  [local(): lax.all_to_all(outbox, 'expert', split_axis=0, concat_axis=0, tiled=True)]
    all_gather x1, waiting for transfers between devices: 41.8 us -> 60.2 us  [local(): lax.all_gather(w_up[0], 'dp', axis=0, tiled=True)]
    select_n x0 -> x1, other arithmetic: none -> 3.39 us  [gather_by_bits(): grown = jnp.where(here & reach == 0, mine_first, theirs_first)]
    ppermute x0 -> x2, starting transfers between devices: none -> 3.03 us  [gather_by_bits(): theirs = lax.ppermute(grown, axis, [(d, d ^ reach) for d in range(ways)])]
  transfers between devices with their start and end apart: 7 -> 8, of which waited for: 5 -> 4; matrix products, arithmetic and copies ran while one was open for 17% -> 20% of each run, Pallas kernels for 0% -> 0%
where the time goes in v1:
time: 268 us; the launch traced here: 267 us
  waiting for transfers between devices  157 us (59%)
  local copies, waits for them, and re-layouts  30.7 us (11%)
  matrix products  24.7 us (9%)
  starting transfers between devices  23.1 us (9%)
  other arithmetic  17.3 us (6%)
  between operations  14.3 us (5%)
    all_gather x1, waiting for transfers between devices, local(): lax.all_gather(w_up[0], 'dp', axis=0, tiled=True)  60.2 us
    ppermute x2, waiting for transfers between devices, gather_by_bits(): theirs = lax.ppermute(grown, axis, [(d, d ^ reach) for d in range(ways)])  36.3 us
    all_to_all x1, waiting for transfers between devices, local(): lax.all_to_all(input_grad, 'expert', split_axis=0, concat_axis=0, tiled=T...  30.5 us
    all_to_all x1, waiting for transfers between devices, local(): lax.all_to_all(expert_out, 'expert', split_axis=0, concat_axis=0, tiled=T...  28.5 us
    scatter x1, local copies, waits for them, and re-layouts, local(): jnp.zeros((groups * capacity, width), jnp.bfloat16).at[slot_place]  6.87 us
    gather x2, local copies, waits for them, and re-layouts, local(): back_grad.reshape(groups * capacity, width)[slot_place].astype(jnp.float32)  6.62 us
    all_to_all x1, starting transfers between devices, local(): lax.all_to_all(outbox, 'expert', split_axis=0, concat_axis=0, tiled=True)  6.48 us
    dot_general x1, matrix products, expert_forward(): jnp.einsum('snf,fd->snd', hidden, down_full, preferred_element_type=jnp.f...  6.27 us
  transfers between devices with their start and end apart: 8, of which 4 were waited for; matrix products, arithmetic and copies ran while one was open for 20% of the time, Pallas kernels for 0%

profile of v1, /device:TPU:0, one launch (start us, length us, event | category | flops | bytes accessed | tf_op | source)
XLA Modules:
  0.0 267.0 jit_solution(14918022140095998716)
XLA Ops:
  7.2 0.0 copy-start
  7.2 0.0 copy-start.5
  7.2 0.0 all-gather.5.cloned.1.call-start
  7.2 0.7 all-gather.5.cloned.1.call-update
  7.9 0.0 all-gather.7.cloned.1.call-start
  8.0 0.7 all-gather.7.cloned.1.call-update
  8.7 0.0 copy-done.5
  8.7 0.1 copy.13
  8.8 0.1 eq.35
  8.9 0.1 eq.31
  9.1 0.1 copy.12
  9.2 0.1 mul.68
  9.4 0.6 reduce-window.6
  9.9 0.2 slice_reduce_fusion
  10.2 0.1 fusion.25
  10.3 0.0 copy-done
  10.3 6.9 %scatter_custom_fusion = bf16[288,2560]{1,0:T(8,128)(2,1)S(1)} fusion(s32[256]{0:T(256)S(1)} %bitcast.35, bf16[128,2560]{1,0:T(8,128)(2,1)S(1)} %copy-done, s32[1024]{0:T(1024)S(1)} %pad_clamp_fusion.1, bf16[]{:T(256)} %constant.31.clone.1), kind=kCustom, calls=%fused_computation.26 | custom fusion | bytes 1474562 | tf_op jit(solution)/shard_map/scatter | solution.py:61
  17.2 1.3 reshape.123
  18.5 6.5 %all-to-all-start = ((bf16[8,36,2560]{2,1,0:T(8,128)(2,1)}), bf16[8,36,2560]{2,1,0:T(8,128)(2,1)}, u32[]{:S(2)}, u32[]{:S(2)}) async-start(bf16[8,36,2560]{2,1,0:T(8,128)(2,1)} %reshape.123), calls=%async_computation | async-start | bytes 3276800 | tf_op jit(solution)/shard_map/all_to_all | solution.py:75
  25.0 0.0 copy-done.4
  25.0 1.6 collective-permute-start
  26.6 36.3 %collective-permute-done = bf16[768,640]{1,0:T(8,128)(2,1)} collective-permute-done((bf16[768,640]{1,0:T(8,128)(2,1)S(1)}, bf16[768,640]{1,0:T(8,128)(2,1)}, u32[]{:S(2)}, u32[]{:S(2)}) %collective-permute-start) | collective-permute-done | bytes 983072 | tf_op jit(solution)/shard_map/ppermute | solution.py:13
  62.9 3.4 %maximum_select_fusion.1 = bf16[768,1280]{1,0:T(8,128)(2,1)} fusion(bf16[768,640]{1,0:T(8,128)(2,1)} %collective-permute-done, bf16[768,640]{1,0:T(8,128)(2,1)S(1)} %bitcast.34, pred[]{:T(512)S(6)} %eq.40), kind=kLoop, calls=%fused_computation.24 | loop fusion | flops 8847360 | bytes 3932161 | tf_op jit(solution)/shard_map/jit(_where)/select_n | solution.py:16
  66.3 1.5 collective-permute-start.1
  67.8 0.0 copy-done.6
  67.8 0.1 copy.11
  67.9 0.1 mul.73
  68.1 1.4 gather_fusion.1
  69.5 2.9 %scatter_custom_fusion.1 = bf16[288,2560]{1,0:T(8,128)(2,1)S(1)} fusion(s32[256]{0:T(256)S(1)} %bitcast.36, bf16[256,2560]{1,0:T(8,128)(2,1)S(1)} %gather_fusion.1, f32[256]{0:T(256)S(1)} %mul.73, bf16[]{:T(256)} %constant.31.clone.1), kind=kCustom, calls=%fused_computation.25 | custom fusion | flops 1966080 | bytes 2786306 | tf_op jit(solution)/shard_map/scatter | solution.py:67
  72.5 1.4 reshape.125
  73.8 0.0 all-to-all-done
  73.8 4.7 %all-to-all-start.2 = ((bf16[8,36,2560]{2,1,0:T(8,128)(2,1)}), bf16[8,36,2560]{2,1,0:T(8,128)(2,1)}, u32[]{:S(2)}, u32[]{:S(2)}) async-start(bf16[8,36,2560]{2,1,0:T(8,128)(2,1)} %reshape.125), calls=%async_computation.2 | async-start | bytes 3276800 | tf_op jit(solution)/shard_map/all_to_all | solution.py:82
  78.5 0.0 all-gather.5.cloned.1.call-done
  78.6 4.1 %fusion.7 = f32[8,36,768]{2,1,0:T(8,128)S(1)} fusion(bf16[8,36,2560]{2,1,0:T(8,128)(2,1)} %all-to-all-done, bf16[1,2560,768]{2,1,0:T(8,128)(2,1)} %all-gather.5.cloned.1.call-done), kind=kOutput, calls=%fused_computation.16 | convolution fusion | flops 1132462080 | bytes 6291456 | tf_op jit(solution)/shard_map/snd,df->snf/dot_general | solution.py:22
  82.6 60.2 %all-gather.7.cloned.1.call-done = bf16[1,2560,768]{2,1,0:T(8,128)(2,1)} async-done(((bf16[1,640,768]{2,1,0:T(8,128)(2,1)}), bf16[1,2560,768]{2,1,0:T(8,128)(2,1)}) %all-gather.7.cloned.1.call-update) | async-done | bytes 3932176 | tf_op jit(solution)/shard_map/all_gather | solution.py:71
  142.8 4.1 %fusion.3 = f32[8,36,768]{2,1,0:T(8,128)S(1)} fusion(bf16[8,36,2560]{2,1,0:T(8,128)(2,1)} %all-to-all-done, bf16[1,2560,768]{2,1,0:T(8,128)(2,1)} %all-gather.7.cloned.1.call-done), kind=kOutput, calls=%fused_computation.12 | convolution fusion | flops 1132462080 | bytes 6291456 | tf_op jit(solution)/shard_map/snd,df->snf/dot_general | solution.py:23
  146.9 0.0 collective-permute-done.1
  146.9 0.9 copy-done.9
  147.8 6.3 %convolution_convert_fusion = bf16[8,36,2560]{2,1,0:T(8,128)(2,1)} fusion(bf16[768,1280]{1,0:T(8,128)(2,1)} %collective-permute-done.1, bf16[768,1280]{1,0:T(8,128)(2,1)} %maximum_select_fusion.1, pred[]{:T(512)S(6)} %eq.39, f32[8,36,768]{2,1,0:T(8,128)S(1)} %fusion.3, f32[8,36,768]{2,1,0:T(8,128)S(1)} %fusion.7), kind=kOutput, calls=%fused_computation.8 | convolution fusion | flops 1152221184 | bytes 7176193 | tf_op jit(solution)/shard_map/snf,fd->snd/dot_general | solution.py:25
  154.1 0.0 all-to-all-done.2
  154.1 4.5 %all-to-all-start.1 = ((bf16[8,36,2560]{2,1,0:T(8,128)(2,1)}), bf16[8,36,2560]{2,1,0:T(8,128)(2,1)}, u32[]{:S(2)}, u32[]{:S(2)}) async-start(bf16[8,36,2560]{2,1,0:T(8,128)(2,1)} %convolution_convert_fusion), calls=%async_computation.1 | async-start | bytes 3276800 | tf_op jit(solution)/shard_map/all_to_all | solution.py:80
  158.6 0.0 copy-start.7
  158.6 0.0 copy-start.10
  158.6 5.8 %fusion.11 = f32[8,36,768]{2,1,0:T(8,128)S(1)} fusion(bf16[8,36,2560]{2,1,0:T(8,128)(2,1)} %all-to-all-done.2, bf16[768,1280]{1,0:T(8,128)(2,1)} %collective-permute-done.1, bf16[768,1280]{1,0:T(8,128)(2,1)} %maximum_select_fusion.1, pred[]{:T(512)S(6)} %eq.39), kind=kOutput, calls=%fused_computation.23 | convolution fusion | flops 1150156800 | bytes 6291457 | tf_op jit(solution)/shard_map/snd,fd->snf/dot_general | solution.py:32
  164.5 0.0 copy-done.7
  164.5 0.0 copy-done.10
  164.5 0.0 copy-start.8
  164.5 1.7 fusion.5
  166.2 0.4 copy-done.8
  166.6 2.7 %fusion = bf16[8,36,2560]{2,1,0:T(8,128)(2,1)} fusion(f32[8,36,2560]{2,1,0:T(8,128)S(1)} %fusion.5, bf16[1,2560,768]{2,1,0:T(8,128)(2,1)S(1)} %copy-done.8, f32[8,36,768]{2,1,0:T(8,128)S(1)} %fusion.11, f32[8,36,768]{2,1,0:T(8,128)S(1)} %fusion.7), kind=kOutput, calls=%fused_computation.7 | convolution fusion | flops 1135263744 | bytes 10125312 | tf_op jit(solution)/shard_map/snf,df->snd/dot_general | solution.py:41
  169.4 28.5 %all-to-all-done.1 = bf16[8,36,2560]{2,1,0:T(8,128)(2,1)} async-done(((bf16[8,36,2560]{2,1,0:T(8,128)(2,1)}), bf16[8,36,2560]{2,1,0:T(8,128)(2,1)}, u32[]{:S(2)}, u32[]{:S(2)}) %all-to-all-start.1) | async-done | bytes 1474592 | tf_op jit(solution)/shard_map/all_to_all | solution.py:80
  197.8 4.3 %all-to-all-start.3 = ((bf16[8,36,2560]{2,1,0:T(8,128)(2,1)}), bf16[8,36,2560]{2,1,0:T(8,128)(2,1)}, u32[]{:S(2)}, u32[]{:S(2)}) async-start(bf16[8,36,2560]{2,1,0:T(8,128)(2,1)} %fusion), calls=%async_computation.3 | async-start | bytes 3276800 | tf_op jit(solution)/shard_map/all_to_all | solution.py:84
  202.2 1.6 reshape.124
  203.7 2.5 gather_fusion
  206.3 4.2 %reshape.128 = f32[128,2,2560]{2,1,0:T(2,128)} reshape(bf16[256,2560]{1,0:T(8,128)(2,1)} %gather_fusion) | data formatting | bytes 3932160 | tf_op jit(solution)/shard_map/convert_element_type | solution.py:85
  210.5 0.4 fusion.10
  210.9 30.5 %all-to-all-done.3 = bf16[8,36,2560]{2,1,0:T(8,128)(2,1)} async-done(((bf16[8,36,2560]{2,1,0:T(8,128)(2,1)}), bf16[8,36,2560]{2,1,0:T(8,128)(2,1)}, u32[]{:S(2)}, u32[]{:S(2)}) %all-to-all-start.3) | async-done | bytes 1474592 | tf_op jit(solution)/shard_map/all_to_all | solution.py:84
  241.4 1.5 reshape.126
  242.9 2.5 gather_fusion.2
  245.5 4.1 %gather.18 = bf16[128,2,2560]{2,1,0:T(2,128)(2,1)} reshape(bf16[256,2560]{1,0:T(8,128)(2,1)} %gather_fusion.2) | data formatting | bytes 2621440 | tf_op jit(solution)/shard_map/gather | solution.py:90
  249.6 5.3 %reduce_sum.44 = bf16[128,2560]{1,0:T(8,128)(2,1)} reduce(bf16[128,2,2560]{2,1,0:T(2,128)(2,1)} %gather.18, bf16[]{:T(256)} %constant.31.clone.1), dimensions={1}, to_apply=%region_6.7 | reduce | flops 327680 | bytes 1966082 | tf_op jit(solution)/shard_map/reduce_sum | solution.py:91
  254.9 0.1 reshape.127
  255.0 0.6 copy.16
  255.7 4.5 %multiply_reduce_fusion = bf16[128,2560]{1,0:T(8,128)(2,1)} fusion(f32[128,2,2560]{2,1,0:T(2,128)S(1)} %copy-done.3, f32[128,2]{1,0:T(8,128)S(1)} %copy.11), kind=kLoop, calls=%fused_computation.22 | loop fusion | flops 983040 | bytes 3277824 | tf_op jit(solution)/shard_map/reduce_sum | solution.py:86
  (17 shorter events, 0.1 us)
Async XLA Ops:
  7.2 3.2 %copy-start = (bf16[128,2560]{1,0:T(8,128)(2,1)S(1)}, bf16[128,2560]{1,0:T(8,128)(2,1)}, u32[]{:S(2)}) copy-start(bf16[128,2560]{1,0:T(8,128)(2,1)} %param.7) | copy-start | bytes 1966084
  7.2 1.5 copy-start.5
  7.2 71.4 %all-gather.5.cloned.1.call-start = ((), (), s32[]{:S(2)}) async-start(), calls=%async_computation.4 | async-start | bytes 4915200 | tf_op jit(solution)/shard_map/all_gather | solution.py:70
  7.9 134.9 %all-gather.7.cloned.1.call-start = ((), (), s32[]{:S(2)}) async-start(), calls=%async_computation.5 | async-start | bytes 4915200 | tf_op jit(solution)/shard_map/all_gather | solution.py:71
  18.5 6.5 %copy-start.4 = (bf16[1,768,640]{2,1,0:T(8,128)(2,1)S(1)}, bf16[1,768,640]{2,1,0:T(8,128)(2,1)}, u32[]{:S(2)}) copy-start(bf16[1,768,640]{2,1,0:T(8,128)(2,1)} %param.12) | copy-start | bytes 2949124
  18.5 55.3 %all-to-all-start = ((bf16[8,36,2560]{2,1,0:T(8,128)(2,1)}), bf16[8,36,2560]{2,1,0:T(8,128)(2,1)}, u32[]{:S(2)}, u32[]{:S(2)}) async-start(bf16[8,36,2560]{2,1,0:T(8,128)(2,1)} %reshape.123), calls=%async_computation | async-start | bytes 3276800 | tf_op jit(solution)/shard_map/all_to_all | solution.py:75
  25.0 37.9 %collective-permute-start = (bf16[768,640]{1,0:T(8,128)(2,1)S(1)}, bf16[768,640]{1,0:T(8,128)(2,1)}, u32[]{:S(2)}, u32[]{:S(2)}) collective-permute-start(bf16[768,640]{1,0:T(8,128)(2,1)S(1)} %bitcast.33), channel_id=1, source_target_pairs={{0,8},{8,0},{16,24},{24,16},{1,9},{9,1},{17,25},{25,17},{2,10},{10... | collective-permute-start | bytes 2949128 | tf_op jit(solution)/shard_map/ppermute | solution.py:13
  26.6 41.2 %copy-start.6 = (f32[128,2]{0,1:T(2,128)S(1)}, f32[128,2]{0,1:T(2,128)}, u32[]{:S(2)}) copy-start(f32[128,2]{0,1:T(2,128)} %param.9) | copy-start | bytes 3076
  26.6 41.5 %copy-start.1 = (bf16[128,2560]{1,0:T(8,128)(2,1)S(1)}, bf16[128,2560]{1,0:T(8,128)(2,1)}, u32[]{:S(2)}) copy-start(bf16[128,2560]{1,0:T(8,128)(2,1)} %param.13) | copy-start | bytes 1966084
  66.3 80.5 %collective-permute-start.1 = (bf16[768,1280]{1,0:T(8,128)(2,1)}, bf16[768,1280]{1,0:T(8,128)(2,1)}, u32[]{:S(2)}, u32[]{:S(2)}) collective-permute-start(bf16[768,1280]{1,0:T(8,128)(2,1)} %maximum_select_fusion.1), channel_id=1, source_target_pairs={{0,16},{8,24},{16,0},{24,8},{1,17},{9,25},{17,1},{25,9},{2,18},{10... | collective-permute-start | bytes 5898248 | tf_op jit(solution)/shard_map/ppermute | solution.py:13
  73.8 80.3 %all-to-all-start.2 = ((bf16[8,36,2560]{2,1,0:T(8,128)(2,1)}), bf16[8,36,2560]{2,1,0:T(8,128)(2,1)}, u32[]{:S(2)}, u32[]{:S(2)}) async-start(bf16[8,36,2560]{2,1,0:T(8,128)(2,1)} %reshape.125), calls=%async_computation.2 | async-start | bytes 3276800 | tf_op jit(solution)/shard_map/all_to_all | solution.py:82
  146.9 0.9 copy-start.9
  154.1 43.8 %all-to-all-start.1 = ((bf16[8,36,2560]{2,1,0:T(8,128)(2,1)}), bf16[8,36,2560]{2,1,0:T(8,128)(2,1)}, u32[]{:S(2)}, u32[]{:S(2)}) async-start(bf16[8,36,2560]{2,1,0:T(8,128)(2,1)} %convolution_convert_fusion), calls=%async_computation.1 | async-start | bytes 3276800 | tf_op jit(solution)/shard_map/all_to_all | solution.py:80
  158.6 5.9 %copy-start.7 = (bf16[1,2560,768]{2,1,0:T(8,128)(2,1)S(1)}, bf16[1,2560,768]{2,1,0:T(8,128)(2,1)}, u32[]{:S(2)}) copy-start(bf16[1,2560,768]{2,1,0:T(8,128)(2,1)} %all-gather.5.cloned.1.call-done) | copy-start | bytes 11796484
  158.6 5.9 %copy-start.10 = (f32[8,36,768]{2,1,0:T(8,128)S(1)}, f32[8,36,768]{2,1,0:T(8,128)}, u32[]{:S(2)}) copy-start(f32[8,36,768]{2,1,0:T(8,128)} %copy-done.9) | copy-start | bytes 2654212
  164.5 2.1 copy-start.8
  197.8 43.5 %all-to-all-start.3 = ((bf16[8,36,2560]{2,1,0:T(8,128)(2,1)}), bf16[8,36,2560]{2,1,0:T(8,128)(2,1)}, u32[]{:S(2)}, u32[]{:S(2)}) async-start(bf16[8,36,2560]{2,1,0:T(8,128)(2,1)} %fusion), calls=%async_computation.3 | async-start | bytes 3276800 | tf_op jit(solution)/shard_map/all_to_all | solution.py:84
  206.3 4.2 %copy-start.2 = (bf16[256,2560]{1,0:T(8,128)(2,1)S(1)}, bf16[256,2560]{1,0:T(8,128)(2,1)}, u32[]{:S(2)}) copy-start(bf16[256,2560]{1,0:T(8,128)(2,1)} %gather_fusion) | copy-start | bytes 3932164
  245.5 10.2 %copy-start.3 = (f32[128,2,2560]{2,1,0:T(2,128)S(1)}, f32[128,2,2560]{2,1,0:T(2,128)}, u32[]{:S(2)}) copy-start(f32[128,2,2560]{2,1,0:T(2,128)} %reshape.128) | copy-start | bytes 7864324
Sparse Core Ops, SparseCore 0:
  9.9 66.0 all-gather.4
  77.8 64.9 all-gather.6
